TPU v7x, 32 devices: a whole 2x2x4 slice. The times are simulated.
32 devices in a mesh: rep: 2 (over x), expert: 8 (over z, y), head: 2 (over core).
Axes of the slice: x: 2, y: 2, z: 4, core: 2. Of those that a mesh axis runs over, the one named last changes fastest.
Arguments:
- hidden_in: bfloat16 [256, 3072], P('rep', ('expert', 'head')), parts along dimension 0, may hold values from -7 to 7
- queries: bfloat16 [256, 4, 6, 128], P(('rep', 'expert'), 'head'), parts along dimension 0, may hold values from -18 to 18, as said below
- new_keys: bfloat16 [256, 4, 128], P(('rep', 'expert'), 'head'), parts along dimension 0, may hold values from -4 to 4
- new_values: bfloat16 [256, 4, 128], P(('rep', 'expert'), 'head'), parts along dimension 0, may hold values from -4 to 4
- cache_keys: bfloat16 [256, 4, 64, 128], P(('rep', 'expert'), 'head'), parts along dimension 0, may hold values from -18 to 18, as said below
- cache_values: bfloat16 [256, 4, 64, 128], P(('rep', 'expert'), 'head'), parts along dimension 0, may hold values from -4 to 4
- parents: int32 [256], P(('rep', 'expert')), parts along dimension 0, may hold values from 0 to 7
- lengths: int32 [32], P(('rep', 'expert')), parts along dimension 0, may hold values from 2 to 64, as said below
- out_proj: bfloat16 [3072, 3072], P(None, ('expert', 'head')), may hold values from -0.109375 to 0.109375
- ffn_gain: float32 [3072], replicated, may hold values from 0.1 to 1.9
- routes: int32 [256, 2], P('rep'), parts along dimension 0, may hold values from 0 to 3, all different within a row; in each aligned block of 128 rows (0 to 127, 128 to 255, ...) at most 80 rows name the same one
- route_weights: float32 [256, 2], P('rep'), parts along dimension 0, may hold values from 0.2 to 1
- w_gate: bfloat16 [3072, 32768], P(None, ('expert', 'head')), may hold values from -0.109375 to 0.109375
- w_up: bfloat16 [3072, 32768], P(None, ('expert', 'head')), may hold values from -0.109375 to 0.109375
- w_down: bfloat16 [32768, 3072], P(('expert', 'head')), may hold values from -0.0625 to 0.0625
- lm_gain: float32 [3072], replicated, may hold values from 0.1 to 1.9
- vocab_weight: bfloat16 [3072, 16384], P(None, ('expert', 'head')), may hold values from -1 to 1
Outputs:
- layer_out: bfloat16 [256, 3072], P('rep', ('expert', 'head')), parts along dimension 0
- best_logits: float32 [256, 8], P('rep'), parts along dimension 0
There are 2 independent parts, one for each index of `rep`. A program takes and returns all parts, laid end to end along the dimension named above; an argument that names none is the same for every part. Nothing has to cross between parts.
Inputs may be any that keep to these rules, and one draw needn't show every extreme that they name: `queries`: in the shown draw entries are truncated normal; values always lie in the printed range. `cache_keys`: in the shown draw entries are truncated normal; values always lie in the printed range. `lengths`: some sequence has exactly 64 cached positions. `routes`: each row names two different experts; no expert is named by more than 80 rows, and one is named by exactly 80.
All inputs are finite; a program needn't handle non-finite values.
Results may differ from a plain program's by a relative error of at most 0.0065.
Values may be sent and summed in bfloat16 or wider, within the bound.
A program may use at most 128 MiB of HBM per device.

v0:
```python
import math

import jax
import jax.numpy as jnp
from jax import lax
from jax.sharding import PartitionSpec as P

E = 4
BEAM = 8
TOPK = 8


def rms_scale(rows, gain):
    values = rows.astype(jnp.float32)
    square_mean = jnp.mean(values * values, axis=-1, keepdims=True)
    return (values * lax.rsqrt(square_mean + 1e-05) * gain).astype(jnp.bfloat16)


def attend(queries, new_keys, new_values, cache_keys, cache_values, parents, lengths):
    row_count = queries.shape[0]
    beam_base = jnp.arange(row_count, dtype=jnp.int32) // BEAM * BEAM
    source = beam_base + parents
    picked_keys = jnp.take(cache_keys, source, axis=0)
    picked_values = jnp.take(cache_values, source, axis=0)
    factor = 1.0 / math.sqrt(queries.shape[-1])
    scores = (
        jnp.einsum("rgjd,rgtd->rgjt", queries, picked_keys, preferred_element_type=jnp.float32)
        * factor
    )
    fresh_score = (
        jnp.einsum("rgjd,rgd->rgj", queries, new_keys, preferred_element_type=jnp.float32) * factor
    )
    limits = jnp.repeat(lengths, BEAM)
    in_cache = jnp.arange(cache_keys.shape[2], dtype=jnp.int32)[None, :] < limits[:, None]
    scores = jnp.where(in_cache[:, None, None, :], scores, -1e30)
    highest = jnp.maximum(jnp.max(scores, axis=-1), fresh_score)
    expo = jnp.exp(scores - highest[..., None])
    own_term = jnp.exp(fresh_score - highest)
    denominator = jnp.sum(expo, axis=-1) + own_term
    weights = (expo / denominator[..., None]).astype(jnp.bfloat16)
    own_weight = (own_term / denominator).astype(jnp.bfloat16)
    context = jnp.einsum(
        "rgjt,rgtd->rgjd", weights, picked_values, preferred_element_type=jnp.float32
    )
    context = (
        context
        + own_weight.astype(jnp.float32)[..., None] * new_values.astype(jnp.float32)[:, :, None, :]
    )
    return context.astype(jnp.bfloat16).reshape(row_count, -1)


def place_slots(routes, capacity):
    row_count = routes.shape[0]
    flat_expert = routes.reshape(-1)
    onehot = (flat_expert[:, None] == jnp.arange(E, dtype=jnp.int32)[None, :]).astype(jnp.int32)
    before = jnp.cumsum(onehot, axis=0) - onehot
    slot_index = jnp.sum(before * onehot, axis=1)
    row_ids = jnp.arange(2 * row_count, dtype=jnp.int32) // 2
    slot_table = (
        jnp.full((E, capacity), row_count, jnp.int32).at[flat_expert, slot_index].set(row_ids)
    )
    return (flat_expert, slot_index, slot_table)


def shards(
    hidden_in,
    queries,
    new_keys,
    new_values,
    cache_keys,
    cache_values,
    parents,
    lengths,
    out_proj,
    ffn_gain,
    routes,
    route_weights,
    w_gate,
    w_up,
    w_down,
    lm_gain,
    vocab_weight,
):
    n_head = lax.axis_size("head")
    n_devices = lax.axis_size("expert") * n_head
    local_rows = queries.shape[0]
    total_rows, col_width = hidden_in.shape
    full_width = col_width * n_devices
    slices = n_devices // E
    capacity = total_rows * 5 // 8
    context = attend(queries, new_keys, new_values, cache_keys, cache_values, parents, lengths)
    head_cols = context.shape[1]
    piece = lax.all_gather(context[None], ("expert", "head"), axis=0, tiled=True)

    def add_piece(step_index, current):
        owner = step_index // n_head
        core_half = step_index % n_head
        context_block = lax.dynamic_index_in_dim(piece, step_index, 0, keepdims=False)
        proj_rows = lax.dynamic_slice_in_dim(out_proj, core_half * head_cols, head_cols, 0)
        product = jnp.dot(context_block, proj_rows, preferred_element_type=jnp.float32)
        first_row = owner * local_rows
        earlier = lax.dynamic_slice_in_dim(current, first_row, local_rows, 0)
        return lax.dynamic_update_slice_in_dim(current, earlier + product, first_row, 0)

    attention = lax.fori_loop(
        0, piece.shape[0], add_piece, jnp.zeros((total_rows, col_width), jnp.float32)
    )
    residual = (hidden_in.astype(jnp.float32) + attention).astype(jnp.bfloat16)
    flat_expert, slot_index, slot_table = place_slots(routes, capacity)
    padded = jnp.concatenate([residual, jnp.zeros((1, col_width), jnp.bfloat16)], axis=0)
    buffers = jnp.take(padded, slot_table.reshape(-1), axis=0).reshape(E, 1, capacity, col_width)
    outgoing = jnp.broadcast_to(buffers, (E, slices, capacity, col_width)).reshape(
        n_devices, capacity, 1, col_width
    )
    arrived = lax.all_to_all(outgoing, ("expert", "head"), split_axis=0, concat_axis=2, tiled=True)
    count_here = arrived.shape[1]
    normed = rms_scale(arrived.reshape(count_here, full_width), ffn_gain)
    gate_proj = jnp.dot(normed, w_gate, preferred_element_type=jnp.float32)
    up_proj = jnp.dot(normed, w_up, preferred_element_type=jnp.float32)
    hidden = (jax.nn.silu(gate_proj) * up_proj).astype(jnp.bfloat16)
    partial_value = jnp.dot(hidden, w_down, preferred_element_type=jnp.float32).astype(jnp.bfloat16)
    count_here = partial_value.shape[0]
    outgoing = partial_value.reshape(count_here, n_devices, 1, col_width)
    returned_rows = lax.all_to_all(
        outgoing, ("expert", "head"), split_axis=1, concat_axis=2, tiled=True
    )
    expert_sums = (
        returned_rows.reshape(capacity, E, slices, col_width).astype(jnp.float32).sum(axis=2)
    )
    picked = expert_sums[slot_index, flat_expert].reshape(total_rows, 2, col_width)
    expert_mix = jnp.sum(route_weights[:, :, None] * picked, axis=1)
    layer_out = (residual.astype(jnp.float32) + expert_mix).astype(jnp.bfloat16)
    gathered = lax.all_gather(layer_out, ("expert", "head"), axis=1, tiled=True)
    final = rms_scale(gathered, lm_gain)
    logits = jnp.dot(final, vocab_weight, preferred_element_type=jnp.float32)
    local_best = lax.top_k(logits, TOPK)[0]
    every_best = lax.all_gather(local_best, ("expert", "head"), axis=1, tiled=True)
    best_logits = lax.top_k(every_best, TOPK)[0]
    return (layer_out, best_logits)


def solution(mesh):
    placed = (
        P("rep", ("expert", "head")),
        P(("rep", "expert"), "head", None, None),
        P(("rep", "expert"), "head", None),
        P(("rep", "expert"), "head", None),
        P(("rep", "expert"), "head", None, None),
        P(("rep", "expert"), "head", None, None),
        P(("rep", "expert")),
        P(("rep", "expert")),
        P(None, ("expert", "head")),
        P(),
        P("rep", None),
        P("rep", None),
        P(None, ("expert", "head")),
        P(None, ("expert", "head")),
        P(("expert", "head"), None),
        P(),
        P(None, ("expert", "head")),
    )
    return jax.shard_map(
        shards,
        mesh=mesh,
        in_specs=placed,
        out_specs=(P("rep", ("expert", "head")), P("rep", None)),
        check_vma=False,
    )
```

profile of v0, /device:TPU:0, one launch (start us, length us, event | category | flops | bytes accessed | tf_op | source)
XLA Modules:
  0.0 201.8 jit_solution(11727125868150128725)
XLA Ops:
  0.7 0.9 copy.54
  2.0 1.2 reduce-window.6
  3.7 11.4 %scatter_fusion = s32[4,80]{1,0:T(4,128)S(1)} fusion(s32[4,80]{1,0:T(4,128)S(1)} %broadcast_in_dim.66, s32[256]{0:T(256)S(1)} %bitcast.53, s32[256]{0:T(256)S(1)} %and_select_fusion), kind=kCustom, calls=%fused_computation.4 | custom fusion | bytes 5120 | tf_op jit(solution)/shard_map/scatter | solution.py:60
  15.2 0.7 broadcast_in_dim.40
  16.0 0.7 compare_and_fusion
  16.8 0.7 convert_element_type.80
  17.5 0.9 copy.51
  18.4 0.6 gather_fusion.3
  19.1 1.7 gather_fusion.2
  20.8 1.0 fusion.25
  21.8 1.3 fusion.44
  23.8 25.5 %all_gather.9 = bf16[16,16,1536]{2,1,0:T(8,128)(2,1)S(1)} all-gather(bf16[1,16,1536]{2,1,0:T(8,128)(2,1)S(1)} %broadcast_in_dim_reshape.2), channel_id=1, replica_groups=mesh['rep'=2,'expert'=8,'head'=2] {'expert','head'}, dimensions={0}, use_global_device_ids=true | all-gather | bytes 835584 | tf_op jit(solution)/shard_map/all_gather | solution.py:93
  49.3 4.4 %while.15 = (s32[]{:T(128)}, f32[128,192]{1,0:T(8,128)S(1)}, bf16[16,16,1536]{2,1,0:T(8,128)(2,1)S(1)}, bf16[3072,192]{0,1:T(8,128)(2,1)S(1)}, s32[]{:T(128)}, /...) while((s32[]{:T(128)}, f32[128,192]{1,0:T(8,128)S(1)}, ...), condition=%wide.region_3.5_spmd, body=%wide.region_2.4_spmd.sunk | while | flops 9440278 | bytes 672088 | solution.py:105
  53.7 2.0 gather_fusion
  55.9 20.8 %all_to_all.8 = bf16[16,80,1,192]{3,1,2,0:T(8,128)(2,1)S(1)} all-to-all(bf16[16,80,1,192]{3,1,2,0:T(8,128)(2,1)S(1)} %bitcast.55), channel_id=1, replica_groups=mesh['rep'=2,'expert'=8,'head'=2] {'expert','head'}, dimensions={0} | all-to-all | bytes 983040 | tf_op jit(solution)/shard_map/all_to_all | solution.py:115
  77.1 0.8 copy.59
  77.9 0.5 reshape.192
  78.4 7.0 %fusion.43 = f32[80,2048]{1,0:T(8,128)S(1)} fusion(bf16[3072,2048]{1,0:T(8,128)(2,1)} %param.33, f32[80,3072]{1,0:T(8,128)S(1)} %reshape.192, f32[3072]{0:T(1024)S(1)} %copy-done.3, f32[80]{0:T(128)S(1)} %add_rsqrt_fusion.1), kind=kOutput, calls=%fused_computation.94 | convolution fusion | flops 1007370240 | bytes 14233920 | tf_op jit(solution)/shard_map/dot_general | solution.py:118
  85.4 12.8 %convolution_convert_fusion = bf16[80,3072]{1,0:T(8,128)(2,1)S(1)} fusion(bf16[2048,3072]{1,0:T(8,128)(2,1)} %param.35, bf16[3072,2048]{1,0:T(8,128)(2,1)} %param.34, f32[80,2048]{1,0:T(8,128)S(1)} %fusion.43, f32[80,3072]{1,0:T(8,128)S(1)} %reshape.192, f32[3072]{0:T(1024)S(1)} %copy-done.3, f32[80]{0:T(128)S(1)} %add_rsqrt_fusion.1), kind=kOutput, calls=%fused_computation.11 | convolution fusion | flops 2015232000 | bytes 27308352 | tf_op jit(solution)/shard_map/dot_general | solution.py:121
  98.2 0.7 reshape.190
  98.9 1.0 copy.60
  99.9 3.8 %all-to-all-start.1 = ((bf16[80,16,1,192]{3,0,2,1:T(8,128)(2,1)}), bf16[80,16,1,192]{3,0,2,1:T(8,128)(2,1)S(1)}, u32[]{:S(2)}, u32[]{:S(2)}) async-start(bf16[80,16,1,192]{3,0,2,1:T(8,128)(2,1)} %copy.60), calls=%async_computation.1 | async-start | bytes 1310720 | tf_op jit(solution)/shard_map/all_to_all | solution.py:124
  103.8 16.4 %all-to-all-done.1 = bf16[80,16,1,192]{3,0,2,1:T(8,128)(2,1)S(1)} async-done(((bf16[80,16,1,192]{3,0,2,1:T(8,128)(2,1)}), bf16[80,16,1,192]{3,0,2,1:T(8,128)(2,1)S(1)}, u32[]{:S(2)}, u32[]{:S(2)}) %all-to-all-start.1) | async-done | bytes 491552 | tf_op jit(solution)/shard_map/all_to_all | solution.py:124
  120.6 1.2 gather_fusion.1
  122.0 0.4 multiply_reduce_fusion
  122.5 22.6 %all_gather.10 = bf16[128,3072]{0,1:T(8,128)(2,1)S(1)} all-gather(bf16[128,192]{0,1:T(8,128)(2,1)S(1)} %copy.65), channel_id=1, replica_groups=mesh['rep'=2,'expert'=8,'head'=2] {'expert','head'}, dimensions={1}, use_global_device_ids=true | all-gather | bytes 835584 | tf_op jit(solution)/shard_map/all_gather | solution.py:133
  145.2 0.4 fusion.6
  145.6 4.6 %fusion.13 = f32[128,1024]{1,0:T(8,128)S(1)} fusion(bf16[3072,1024]{1,0:T(8,128)(2,1)} %param.37, bf16[128,3072]{0,1:T(8,128)(2,1)S(1)} %all_gather.10, f32[3072]{0:T(1024)S(1)} %copy-done.4, f32[128]{0:T(128)S(1)} %add_rsqrt_fusion), kind=kOutput, calls=%fused_computation.29 | convolution fusion | flops 806879232 | bytes 7614976 | tf_op jit(solution)/shard_map/dot_general | solution.py:135
  150.2 31.4 %top_k.13 = (f32[128,8]{1,0:T(8,128)S(1)}, s32[128,8]{1,0:T(8,128)}) custom-call(f32[128,1024]{1,0:T(8,128)S(1)} %fusion.13), custom_call_target="TopK", called_computations={%compare_greater_than.1.14.clone.clone} | custom-call | tf_op jit(solution)/shard_map/top_k | solution.py:136
  181.6 17.6 %all_gather.11 = f32[128,128]{0,1:T(8,128)S(1)} all-gather(f32[128,8]{0,1:T(8,128)S(1)} %copy.63), channel_id=1, replica_groups=mesh['rep'=2,'expert'=8,'head'=2] {'expert','head'}, dimensions={1}, use_global_device_ids=true | all-gather | bytes 69632 | tf_op jit(solution)/shard_map/all_gather | solution.py:137
  199.2 1.8 top_k.14
  201.1 0.7 copy.66
  (72 shorter events, 7.6 us)
Async XLA Ops:
  0.6 17.8 %copy-start = (bf16[16,2,64,128]{3,2,1,0:T(8,128)(2,1)S(1)}, bf16[16,2,64,128]{3,2,1,0:T(8,128)(2,1)}, u32[]{:S(2)}) copy-start(bf16[16,2,64,128]{3,2,1,0:T(8,128)(2,1)} %param.26) | copy-start | bytes 1572868
  0.6 48.6 %copy-start.1 = (bf16[3072,192]{0,1:T(8,128)(2,1)S(1)}, bf16[3072,192]{0,1:T(8,128)(2,1)}, u32[]{:S(2)}) copy-start(bf16[3072,192]{0,1:T(8,128)(2,1)} %param.29) | copy-start | bytes 3538948
  53.7 24.7 %copy-start.3 = (f32[3072]{0:T(1024)S(1)}, f32[3072]{0:T(1024)}, u32[]{:S(2)}) copy-start(f32[3072]{0:T(1024)} %param.30) | copy-start | bytes 36868
  85.4 18.4 %copy-start.5 = (f32[128,2]{0,1:T(2,128)S(1)}, f32[128,2]{0,1:T(2,128)}, u32[]{:S(2)}) copy-start(f32[128,2]{0,1:T(2,128)} %param.32) | copy-start | bytes 3076
  98.1 47.5 %copy-start.4 = (f32[3072]{0:T(1024)S(1)}, f32[3072]{0:T(1024)}, u32[]{:S(2)}) copy-start(f32[3072]{0:T(1024)} %param.36) | copy-start | bytes 36868
  99.9 20.3 %all-to-all-start.1 = ((bf16[80,16,1,192]{3,0,2,1:T(8,128)(2,1)}), bf16[80,16,1,192]{3,0,2,1:T(8,128)(2,1)S(1)}, u32[]{:S(2)}, u32[]{:S(2)}) async-start(bf16[80,16,1,192]{3,0,2,1:T(8,128)(2,1)} %copy.60), calls=%async_computation.1 | async-start | bytes 1310720 | tf_op jit(solution)/shard_map/all_to_all | solution.py:124
  122.5 79.3 %copy-start.2 = (bf16[128,192]{0,1:T(8,128)(2,1)}, bf16[128,192]{0,1:T(8,128)(2,1)S(1)}, u32[]{:S(2)}) copy-start(bf16[128,192]{0,1:T(8,128)(2,1)S(1)} %copy.65) | copy-start | bytes 147460
where the time goes:
time: 202 us
  blocking collectives  86.5 us (43%)
  other arithmetic  37.8 us (19%)
  matrix products  31.3 us (15%)
  local copies, waits for them, and re-layouts  25 us (12%)
  waiting for transfers between devices  16.4 us (8%)
  starting transfers between devices  3.77 us (2%)
    top_k x1, other arithmetic, shards(): local_best = lax.top_k(logits, TOPK)[0]  31.4 us
    all_gather x1, blocking collectives, shards(): lax.all_gather(context[None], ('expert', 'head'), axis=0, tiled=True)  25.5 us
    all_gather x1, blocking collectives, shards(): gathered = lax.all_gather(layer_out, ('expert', 'head'), axis=1, tiled=True)  22.6 us
    all_to_all x1, blocking collectives, shards(): lax.all_to_all(outgoing, ('expert', 'head'), split_axis=0, concat_axis=2,...  20.8 us
    all_gather x1, blocking collectives, shards(): lax.all_gather(local_best, ('expert', 'head'), axis=1, tiled=True)  17.6 us
    all_to_all x1, waiting for transfers between devices, shards(): lax.all_to_all(outgoing, ('expert', 'head'), split_axis=1, concat_axis=2,...  16.4 us
    dot_general x1, matrix products, shards(): jnp.dot(hidden, w_down, preferred_element_type=jnp.float32)  12.8 us
    scatter x1, local copies, waits for them, and re-layouts, place_slots(): jnp.full((E, capacity), row_count, jnp.int32).at[flat_expert, slot_index]  11.4 us
  transfers between devices with their start and end apart: 1, of which 1 were waited for; matrix products, arithmetic and copies ran while one was open for 0% of the time, Pallas kernels for 0%

commit v1 on v0

v1 whole, which is shorter than its diff:
```python
import functools
import math

import jax
import jax.numpy as jnp
from jax import lax
from jax.experimental import pallas as pl
from jax.experimental.pallas import tpu as pltpu
from jax.sharding import PartitionSpec as P

E = 4
BEAM = 8
TOPK = 8


def attend(queries, new_keys, new_values, cache_keys, cache_values, parents, lengths):
    row_count = queries.shape[0]
    beam_base = jnp.arange(row_count, dtype=jnp.int32) // BEAM * BEAM
    source = beam_base + parents
    picked_keys = jnp.take(cache_keys, source, axis=0)
    picked_values = jnp.take(cache_values, source, axis=0)
    factor = 1.0 / math.sqrt(queries.shape[-1])
    scores = (
        jnp.einsum("rgjd,rgtd->rgjt", queries, picked_keys, preferred_element_type=jnp.float32)
        * factor
    )
    fresh_score = (
        jnp.einsum("rgjd,rgd->rgj", queries, new_keys, preferred_element_type=jnp.float32) * factor
    )
    limits = jnp.repeat(lengths, BEAM)
    in_cache = jnp.arange(cache_keys.shape[2], dtype=jnp.int32)[None, :] < limits[:, None]
    scores = jnp.where(in_cache[:, None, None, :], scores, -1e30)
    highest = jnp.maximum(jnp.max(scores, axis=-1), fresh_score)
    expo = jnp.exp(scores - highest[..., None])
    own_term = jnp.exp(fresh_score - highest)
    denominator = jnp.sum(expo, axis=-1) + own_term
    weights = (expo / denominator[..., None]).astype(jnp.bfloat16)
    own_weight = (own_term / denominator).astype(jnp.bfloat16)
    context = jnp.einsum(
        "rgjt,rgtd->rgjd", weights, picked_values, preferred_element_type=jnp.float32
    )
    context = (
        context
        + own_weight.astype(jnp.float32)[..., None] * new_values.astype(jnp.float32)[:, :, None, :]
    )
    return context.astype(jnp.bfloat16).reshape(row_count, -1)


TILE = 256
MESH = pl.DeviceIdType.MESH


def aligned(index, size):
    return pl.ds(pl.multiple_of(index * size, size), size)


def best_of(source, groups, width):
    def insert(group, kept):
        item = source[aligned(group, 8), :]
        result = []
        for level in kept:
            result.append(jnp.maximum(level, item))
            item = jnp.minimum(level, item)
        return tuple(result)

    lowest = jnp.full((8, width), -jnp.inf, jnp.float32)
    kept = list(lax.fori_loop(0, groups, insert, (lowest,) * TOPK))
    lane_class = lax.broadcasted_iota(jnp.int32, (8, width), 0)
    best = []
    for _ in range(TOPK):
        top = jnp.max(kept[0], axis=0, keepdims=True)
        first = jnp.min(jnp.where(kept[0] == top, lane_class, 8), axis=0, keepdims=True)
        taken = lane_class == first
        best.append(top)
        kept = [
            jnp.where(taken, kept[j + 1] if j + 1 < TOPK else lowest, kept[j])
            for j in range(TOPK)
        ]
    return best


def layer_kernel(
    n_expert,
    n_head,
    context_ref,
    proj_ref,
    hidden_ref,
    ffn_gain_ref,
    routes_ref,
    route_weights_ref,
    gate_hbm,
    up_hbm,
    down_hbm,
    lm_gain_ref,
    vocab_hbm,
    layer_ref,
    best_ref,
    gate,
    up,
    down,
    vocab,
    load_sem,
    contexts,
    stream,
    final_stream,
    rows_major,
    hidden,
    partials,
    from_core,
    core_sums,
    from_y,
    y_sums,
    from_z,
    logits,
    candidates,
    send_sem,
    recv_sem,
):
    n_devices = n_expert * n_head
    z_size = n_expert // 2
    e = lax.axis_index("expert")
    h = lax.axis_index("head")
    me = e * n_head + h
    z, y = e // 2, lax.rem(e, 2)
    local_rows = context_ref.shape[0]
    width, rows = hidden_ref.shape
    full_width = width * n_devices
    y_peer = {"expert": z * 2 + 1 - y, "head": h}
    core_peer = {"expert": e, "head": 1 - h}

    loads = [
        pltpu.make_async_copy(source, target, load_sem.at[i])
        for i, (source, target) in enumerate(
            ((gate_hbm, gate), (up_hbm, up), (down_hbm, down), (vocab_hbm, vocab))
        )
    ]
    for load in loads:
        load.start()

    def device(index):
        return {"expert": index // n_head, "head": lax.rem(index, n_head)}

    barrier = pltpu.get_barrier_semaphore()

    def greet(k, carry):
        other = lax.rem(me + k, n_devices)
        pl.semaphore_signal(barrier, inc=1, device_id=device(other), device_id_type=MESH)
        return carry

    lax.fori_loop(1, n_devices, greet, 0)
    pl.semaphore_wait(barrier, n_devices - 1)

    def remote(phase, slot, source, target, device_id):
        return pltpu.make_async_remote_copy(
            src_ref=source,
            dst_ref=target,
            send_sem=send_sem.at[phase, slot],
            recv_sem=recv_sem.at[phase, slot],
            device_id=device_id,
            device_id_type=MESH,
        )

    first_y = z_size - 1
    first_core = 2 * z_size - 1

    def loop(start, stop, step):
        def run(k, carry):
            step(k)
            return carry

        lax.fori_loop(start, stop, run, 0)

    def gather(phase, block):
        def move(slot, expert, head, device_id):
            return remote(phase, slot, block(expert, head), block(expert, head), device_id)

        own = block(e, h)

        def to_z(k):
            target = lax.rem(z + k, z_size) * 2 + y
            move(k - 1, e, h, {"expert": target, "head": h}).start()

        loop(1, z_size, to_z)
        move(first_y, e, h, y_peer).start()
        move(first_core, e, h, core_peer).start()

        def on_z(k):
            expert = lax.rem(z + z_size - k, z_size) * 2 + y
            move(k - 1, expert, h, y_peer).wait_recv()
            move(first_y + k, expert, h, y_peer).start()
            move(first_core + k, expert, h, core_peer).start()

        loop(1, z_size, on_z)

        def on_y(k):
            expert = lax.rem(z + z_size - k, z_size) * 2 + 1 - y
            move(first_y + k, expert, h, y_peer).wait_recv()
            move(first_core + z_size + k, expert, h, core_peer).start()

        loop(0, z_size, on_y)

        def on_core(k):
            move(first_core + k, e, 1 - h, core_peer).wait_recv()

        loop(0, 2 * z_size, on_core)

        def sent(k):
            move(k, e, h, core_peer).wait_send()

        loop(0, n_devices - 1, sent)

    def context_block(expert, head):
        return contexts.at[head, aligned(expert, local_rows)]

    def feature_block(buffer):
        return lambda expert, head: buffer.at[aligned(expert * n_head + head, width)]

    contexts[h, aligned(e, local_rows), :] = context_ref[...]
    gather(0, context_block)
    half = context_ref.shape[1]
    attention = hidden_ref[...].astype(jnp.float32)
    for head in range(n_head):
        attention += lax.dot_general(
            proj_ref[:, head * half : (head + 1) * half],
            contexts[head],
            (((1,), (1,)), ((), ())),
            preferred_element_type=jnp.float32,
        )
    residual = attention.astype(jnp.bfloat16)
    stream[aligned(me, width), :] = residual
    gather(1, feature_block(stream))

    def normalise(source, gain_ref):
        def square(i, total):
            block = source[aligned(i, TILE), :].astype(jnp.float32)
            return total + jnp.sum(block * block, axis=0, keepdims=True)

        total = lax.fori_loop(0, full_width // TILE, square, jnp.zeros((1, rows), jnp.float32))
        scale = lax.rsqrt(total / full_width + 1e-05)

        def turn(i):
            block = source[aligned(i, TILE), :].astype(jnp.float32) * scale
            block = block.T * gain_ref[:, aligned(i, TILE)]
            rows_major[:, aligned(i, TILE)] = block.astype(jnp.bfloat16)

        loop(0, full_width // TILE, turn)

    normalise(stream, ffn_gain_ref)
    loads[0].wait()
    loads[1].wait()

    def widen(i):
        columns = aligned(i, TILE)
        normed = rows_major[...]
        gate_proj = jnp.dot(normed, gate[:, columns], preferred_element_type=jnp.float32)
        up_proj = jnp.dot(normed, up[:, columns], preferred_element_type=jnp.float32)
        active = gate_proj / (1.0 + jnp.exp(-gate_proj)) * up_proj
        hidden[:, columns] = active.astype(jnp.bfloat16)

    loop(0, hidden.shape[1] // TILE, widen)
    loads[2].wait()
    expert_here = me // (n_devices // E)
    share = jnp.sum(
        jnp.where(routes_ref[...] == expert_here, route_weights_ref[...], 0.0),
        axis=0,
        keepdims=True,
    )

    def narrow(i):
        columns = aligned(i, TILE)
        product = jnp.dot(hidden[...], down[:, columns], preferred_element_type=jnp.float32)
        partials[columns, :] = (product.T * share).astype(jnp.bfloat16)

    loop(0, full_width // TILE, narrow)

    mine = feature_block(partials)

    def core_copy(expert):
        return remote(
            2, first_core + expert, mine(expert, 1 - h), from_core.at[expert], core_peer
        )

    def y_copy(k):
        return remote(2, first_y + k, core_sums.at[k * 2 + 1 - y], from_y.at[k], y_peer)

    def z_copy(k):
        target = lax.rem(z + k, z_size)
        return remote(
            2,
            k - 1,
            y_sums.at[target],
            from_z.at[k - 1],
            {"expert": target * 2 + y, "head": h},
        )

    def core_order(k):
        turned = lax.rem(z + 1 + lax.rem(k, z_size), z_size)
        side = k // z_size
        return turned, turned * 2 + lax.rem(1 - y + side, 2)

    def core_start(k):
        core_copy(core_order(k)[1]).start()

    loop(0, n_expert, core_start)

    def core_add(expert):
        core_copy(expert).wait_recv()
        own = partials[aligned(expert * n_head + h, width), :].astype(jnp.float32)
        core_sums[expert] = (own + from_core[expert].astype(jnp.float32)).astype(jnp.bfloat16)

    def core_send(k):
        turned, expert = core_order(k)
        core_add(expert)
        y_copy(turned).start()

    loop(0, z_size, core_send)

    def core_keep(k):
        core_add(core_order(k)[1])

    loop(z_size, n_expert, core_keep)

    def y_add(k):
        y_copy(k).wait_recv()
        total = core_sums[k * 2 + y].astype(jnp.float32) + from_y[k].astype(jnp.float32)
        y_sums[k] = total.astype(jnp.bfloat16)

    def y_send(k):
        y_add(lax.rem(z + k, z_size))
        z_copy(k).start()

    loop(1, z_size, y_send)
    y_add(z)
    total = stream[aligned(me, width), :].astype(jnp.float32) + y_sums[z].astype(jnp.float32)

    def z_add(k, total):
        z_copy(k).wait_recv()
        return total + from_z[k - 1].astype(jnp.float32)

    total = lax.fori_loop(1, z_size, z_add, total)
    layer_out = total.astype(jnp.bfloat16)
    layer_ref[...] = layer_out
    final_stream[aligned(me, width), :] = layer_out
    gather(3, feature_block(final_stream))

    def summed(k):
        core_copy(k).wait_send()

    loop(0, n_expert, summed)
    loop(0, z_size, lambda k: y_copy(k).wait_send())
    loop(1, z_size, lambda k: z_copy(k).wait_send())

    normalise(final_stream, lm_gain_ref)
    loads[3].wait()

    def project(i):
        columns = aligned(i, TILE)
        product = jnp.dot(rows_major[...], vocab[:, columns], preferred_element_type=jnp.float32)
        logits[columns, :] = product.T

    loop(0, logits.shape[0] // TILE, project)
    best = jnp.concatenate(best_of(logits, logits.shape[0] // 8, rows), axis=0)
    candidates[aligned(me, TOPK), :] = best

    def offer(k):
        own = candidates.at[aligned(me, TOPK)]
        return remote(4, k - 1, own, own, device(lax.rem(me + k, n_devices)))

    loop(1, n_devices, lambda k: offer(k).start())
    loop(1, n_devices, lambda k: offer(k).wait_recv())
    best_ref[...] = jnp.concatenate(best_of(candidates, n_devices, rows), axis=0)
    loop(1, n_devices, lambda k: offer(k).wait_send())


def shards(
    hidden_in,
    queries,
    new_keys,
    new_values,
    cache_keys,
    cache_values,
    parents,
    lengths,
    out_proj,
    ffn_gain,
    routes,
    route_weights,
    w_gate,
    w_up,
    w_down,
    lm_gain,
    vocab_weight,
):
    n_head = lax.axis_size("head")
    n_expert = lax.axis_size("expert")
    n_devices = n_expert * n_head
    rows, width = hidden_in.shape
    full_width = width * n_devices
    context = attend(queries, new_keys, new_values, cache_keys, cache_values, parents, lengths)
    in_vmem = pl.BlockSpec(memory_space=pltpu.VMEM)
    in_hbm = pl.BlockSpec(memory_space=pl.ANY)
    half16 = lambda *shape: pltpu.VMEM(shape, jnp.bfloat16)
    layer_t, best_t = pl.pallas_call(
        functools.partial(layer_kernel, n_expert, n_head),
        out_shape=(
            jax.ShapeDtypeStruct((width, rows), jnp.bfloat16),
            jax.ShapeDtypeStruct((TOPK, rows), jnp.float32),
        ),
        in_specs=[in_vmem] * 6 + [in_hbm] * 3 + [in_vmem, in_hbm],
        out_specs=(in_vmem, in_vmem),
        scratch_shapes=[
            half16(*w_gate.shape),
            half16(*w_up.shape),
            half16(*w_down.shape),
            half16(*vocab_weight.shape),
            pltpu.SemaphoreType.DMA((4,)),
            half16(n_head, n_expert * context.shape[0], context.shape[1]),
            half16(full_width, rows),
            half16(full_width, rows),
            half16(rows, full_width),
            half16(rows, w_gate.shape[1]),
            half16(full_width, rows),
            half16(n_expert, width, rows),
            half16(n_expert, width, rows),
            half16(n_expert // 2, width, rows),
            half16(n_expert // 2, width, rows),
            half16(n_expert // 2, width, rows),
            pltpu.VMEM((vocab_weight.shape[1], rows), jnp.float32),
            pltpu.VMEM((n_devices * TOPK, rows), jnp.float32),
            pltpu.SemaphoreType.DMA((5, n_devices - 1)),
            pltpu.SemaphoreType.DMA((5, n_devices - 1)),
        ],
        compiler_params=pltpu.CompilerParams(
            collective_id=0, has_side_effects=True, vmem_limit_bytes=60 * 2**20
        ),
    )(
        context,
        out_proj.T,
        hidden_in.T,
        ffn_gain[None],
        routes.T,
        route_weights.T,
        w_gate,
        w_up,
        w_down,
        lm_gain[None],
        vocab_weight,
    )
    return (layer_t.T, best_t.T)


def solution(mesh):
    placed = (
        P("rep", ("expert", "head")),
        P(("rep", "expert"), "head", None, None),
        P(("rep", "expert"), "head", None),
        P(("rep", "expert"), "head", None),
        P(("rep", "expert"), "head", None, None),
        P(("rep", "expert"), "head", None, None),
        P(("rep", "expert")),
        P(("rep", "expert")),
        P(None, ("expert", "head")),
        P(),
        P("rep", None),
        P("rep", None),
        P(None, ("expert", "head")),
        P(None, ("expert", "head")),
        P(("expert", "head"), None),
        P(),
        P(None, ("expert", "head")),
    )
    return jax.shard_map(
        shards,
        mesh=mesh,
        in_specs=placed,
        out_specs=(P("rep", ("expert", "head")), P("rep", None)),
        check_vma=False,
    )
```

time: 202 us -> 84.1 us (0.42)
  blocking collectives: 86.5 us -> 0 us
  Pallas kernels: 0 us -> 71.7 us
  other arithmetic: 37.8 us -> 1.77 us
  matrix products: 31.3 us -> 2.61 us
  local copies, waits for them, and re-layouts: 25 us -> 6.86 us
  waiting for transfers between devices: 16.4 us -> 0 us
  starting transfers between devices: 3.77 us -> 0 us
    pallas_call x0 -> x1, Pallas kernels: none -> 71.7 us  [shards(): pl.pallas_call(functools.partial(layer_kernel, n_expert, n_head), out_sha...]
    all_gather x3 -> x0, blocking collectives: 65.7 us -> none  [the longest x1 25.5 us: shards(): lax.all_gather(context[None], ('expert', 'head'), axis=0, tiled=True)]
    top_k x2 -> x0, other arithmetic: 33.2 us -> none  [the longest x1 31.4 us: shards(): local_best = lax.top_k(logits, TOPK)[0]]
    dot_general x19 -> x0, matrix products: 28.6 us -> none  [the longest x1 12.8 us: shards(): jnp.dot(hidden, w_down, preferred_element_type=jnp.float32)]
    all_to_all x1 -> x0, blocking collectives: 20.8 us -> none  [shards(): lax.all_to_all(outgoing, ('expert', 'head'), split_axis=0, concat_axis=2,...]
    all_to_all x1 -> x0, waiting for transfers between devices: 16.4 us -> none  [shards(): lax.all_to_all(outgoing, ('expert', 'head'), split_axis=1, concat_axis=2,...]
    scatter x1 -> x0, local copies, waits for them, and re-layouts: 11.4 us -> none  [place_slots(): jnp.full((E, capacity), row_count, jnp.int32).at[flat_expert, slot_index]]
    all_to_all x1 -> x0, starting transfers between devices: 3.77 us -> none  [shards(): lax.all_to_all(outgoing, ('expert', 'head'), split_axis=1, concat_axis=2,...]
  transfers between devices with their start and end apart: 1 -> 0, of which waited for: 1 -> 0; matrix products, arithmetic and copies ran while one was open for 0% -> 0% of each run, Pallas kernels for 0% -> 0%
where the time goes in v1:
time: 84.1 us; the launch traced here: 83.6 us
  Pallas kernels  71.7 us (85%)
  local copies, waits for them, and re-layouts  6.86 us (8%)
  matrix products  2.61 us (3%)
  other arithmetic  1.77 us (2%)
    pallas_call x1, Pallas kernels, shards(): pl.pallas_call(functools.partial(layer_kernel, n_expert, n_head), out_sha...  71.7 us
    unnamed x4, local copies, waits for them, and re-layouts  3.02 us
    gather x1, local copies, waits for them, and re-layouts, attend(): picked_values = jnp.take(cache_values, source, axis=0)  1.69 us

profile of v1, /device:TPU:0, one launch (start us, length us, event | category | flops | bytes accessed | tf_op | source)
XLA Modules:
  0.0 83.6 jit_solution(7392224279809288969)
XLA Ops:
  0.6 0.0 copy-start
  0.6 0.7 compare_and_fusion
  1.4 0.3 copy-done
  1.7 0.6 gather_fusion
  2.3 0.7 broadcast_in_dim.36
  3.1 0.1 lt.23
  3.2 0.1 iota_compare_fusion
  3.2 1.3 %fusion.22 = (f32[16,2,6]{2,1,0:T(2,128)S(1)}, f32[16,2,6,64]{3,2,1,0:T(8,128)S(1)}) fusion(bf16[16,2,6,128]{3,1,2,0:T(2,128)(2,1)} %param.20, bf16[16,2,64,128]{3,2,1,0:T(8,128)(2,1)S(1)} %gather_fusion, pred[16]{0:T(512)(128)(4,1)S(1)} %get-tuple-element.7, pred[16,64]{1,0:T(8,128)(4,1)S(1)} %iota_compare_fusion), kind=kOutput, calls=%fused_computation.39 | convolution fusion | flops 3444544 | bytes 624400 | tf_op jit(solution)/shard_map/rgjd,rgtd->rgjt/dot_general | solution.py:24
  4.6 1.0 %fusion.10 = f32[16,2,1,6]{3,2,1,0:T(1,128)S(1)} fusion(bf16[16,2,6,128]{3,1,2,0:T(2,128)(2,1)} %param.20, bf16[16,2,128,1]{2,1,0,3:T(2,128)(2,1)} %bitcast.23), kind=kOutput, calls=%fused_computation.16 | convolution fusion | flops 49152 | bytes 58112 | tf_op jit(solution)/shard_map/rgjd,rgd->rgj/dot_general | solution.py:28
  5.6 0.2 fusion.9
  5.8 1.7 %gather_fusion.1 = bf16[16,2,64,128]{3,2,1,0:T(8,128)(2,1)S(1)} fusion(bf16[16,2,64,128]{3,2,1,0:T(8,128)(2,1)} %param.24, s32[1024]{0:T(1024)S(1)} %pad_clamp_fusion), kind=kCustom, calls=%fused_computation.1.clone | custom fusion | bytes 1048640 | tf_op jit(solution)/shard_map/jit(_take)/gather | solution.py:21
  7.5 0.7 convert_element_type.18
  8.2 0.3 fusion.2
  8.5 0.7 reshape.36.context_ref
  9.2 71.7 %shard_map.176 = (bf16[192,128]{1,0:T(8,128)(2,1)}, f32[8,128]{1,0:T(8,128)}) custom-call(bf16[16,1536]{1,0:T(8,128)(2,1)} %reshape.36.context_ref, bf16[192,3072]{1,0:T(8,128)(2,1)} %bitcast.13, bf16[192,128]{1,0:T(8,128)(2,1)} %bitcast.16, f32[1,3072]{1,0:T(1,128)} %bitcast.18, s32[2,128]{1,0:T(2,128)} %bitcast.21, f32[2,128]{1,0:T(2,128)} %bitcast.22, ...), custom_call_target="tpu_custom_call" | custom-call | tf_op jit(solution)/shard_map/pallas_call | solution.py:403
  80.9 1.4 %copy.33 = bf16[128,192]{0,1:T(8,128)(2,1)} copy(bf16[128,192]{0,1:T(8,128)(2,1)} %bitcast.17) | data formatting | bytes 98304
  82.4 1.3 %copy.34 = f32[128,8]{0,1:T(8,128)} copy(f32[128,8]{0,1:T(8,128)} %bitcast.20) | data formatting | bytes 8192
  (3 shorter events, 0.1 us)
Async XLA Ops:
  0.6 1.1 %copy-start = (bf16[16,2,64,128]{3,2,1,0:T(8,128)(2,1)S(1)}, bf16[16,2,64,128]{3,2,1,0:T(8,128)(2,1)}, u32[]{:S(2)}) copy-start(bf16[16,2,64,128]{3,2,1,0:T(8,128)(2,1)} %param.23) | copy-start | bytes 1572868

commit v2 on v1

--- a/solution.py
+++ b/solution.py
@@ -103,7 +103,11 @@
     contexts,
     stream,
     final_stream,
-    rows_major,
+    ffn_squares,
+    gate_total,
+    up_total,
+    lm_squares,
+    logit_total,
     hidden,
     partials,
     from_core,
@@ -170,7 +174,7 @@
 
         lax.fori_loop(start, stop, run, 0)
 
-    def gather(phase, block):
+    def gather(phase, block, consume=None):
         def move(slot, expert, head, device_id):
             return remote(phase, slot, block(expert, head), block(expert, head), device_id)
 
@@ -184,25 +188,28 @@
         move(first_y, e, h, y_peer).start()
         move(first_core, e, h, core_peer).start()
 
-        def on_z(k):
-            expert = lax.rem(z + z_size - k, z_size) * 2 + y
-            move(k - 1, expert, h, y_peer).wait_recv()
-            move(first_y + k, expert, h, y_peer).start()
-            move(first_core + k, expert, h, core_peer).start()
-
-        loop(1, z_size, on_z)
-
-        def on_y(k):
-            expert = lax.rem(z + z_size - k, z_size) * 2 + 1 - y
-            move(first_y + k, expert, h, y_peer).wait_recv()
-            move(first_core + z_size + k, expert, h, core_peer).start()
-
-        loop(0, z_size, on_y)
-
-        def on_core(k):
-            move(first_core + k, e, 1 - h, core_peer).wait_recv()
-
-        loop(0, 2 * z_size, on_core)
+        def step(k):
+            @pl.when(jnp.logical_and(k >= 0, k < z_size - 1))
+            def _():
+                expert = lax.rem(z + z_size - k - 1, z_size) * 2 + y
+                move(k, expert, h, y_peer).wait_recv()
+                move(first_y + k + 1, expert, h, y_peer).start()
+                move(first_core + k + 1, expert, h, core_peer).start()
+
+            @pl.when(jnp.logical_and(k >= 0, k < z_size))
+            def _():
+                expert = lax.rem(z + z_size - k, z_size) * 2 + 1 - y
+                move(first_y + k, expert, h, y_peer).wait_recv()
+                move(first_core + z_size + k, expert, h, core_peer).start()
+
+            @pl.when(k >= 1)
+            def _():
+                move(first_core + k - 1, e, 1 - h, core_peer).wait_recv()
+                move(first_core + z_size + k - 1, e, 1 - h, core_peer).wait_recv()
+                if consume is not None:
+                    consume(lax.rem(z + z_size - k + 1, z_size))
+
+        loop(0, z_size + 1, step)
 
         def sent(k):
             move(k, e, h, core_peer).wait_send()
@@ -228,32 +235,45 @@
         )
     residual = attention.astype(jnp.bfloat16)
     stream[aligned(me, width), :] = residual
-    gather(1, feature_block(stream))
-
-    def normalise(source, gain_ref):
-        def square(i, total):
-            block = source[aligned(i, TILE), :].astype(jnp.float32)
-            return total + jnp.sum(block * block, axis=0, keepdims=True)
-
-        total = lax.fori_loop(0, full_width // TILE, square, jnp.zeros((1, rows), jnp.float32))
-        scale = lax.rsqrt(total / full_width + 1e-05)
-
-        def turn(i):
-            block = source[aligned(i, TILE), :].astype(jnp.float32) * scale
-            block = block.T * gain_ref[:, aligned(i, TILE)]
-            rows_major[:, aligned(i, TILE)] = block.astype(jnp.bfloat16)
-
-        loop(0, full_width // TILE, turn)
-
-    normalise(stream, ffn_gain_ref)
+    group = n_head * 2 * width
+
+    def clear(*totals):
+        for total in totals:
+            total[...] = jnp.zeros_like(total)
+
+    def multiply(source, gain_ref, squares, pairs):
+        def consume(number):
+            features = aligned(number, group)
+            block = source[features, :].astype(jnp.float32).T
+            squares[...] += jnp.sum(block * block, axis=1, keepdims=True)
+            block = (block * gain_ref[number]).astype(jnp.bfloat16)
+
+            def tile(i):
+                columns = aligned(i, TILE)
+                for weight, total in pairs:
+                    total[:, columns] += jnp.dot(
+                        block, weight[features, columns], preferred_element_type=jnp.float32
+                    )
+
+            loop(0, pairs[0][0].shape[1] // TILE, tile)
+
+        return consume
+
+    clear(ffn_squares, gate_total, up_total)
     loads[0].wait()
     loads[1].wait()
+    gather(
+        1,
+        feature_block(stream),
+        multiply(stream, ffn_gain_ref, ffn_squares, ((gate, gate_total), (up, up_total))),
+    )
+
+    ffn_scale = lax.rsqrt(ffn_squares[...] / full_width + 1e-05)
 
     def widen(i):
         columns = aligned(i, TILE)
-        normed = rows_major[...]
-        gate_proj = jnp.dot(normed, gate[:, columns], preferred_element_type=jnp.float32)
-        up_proj = jnp.dot(normed, up[:, columns], preferred_element_type=jnp.float32)
+        gate_proj = gate_total[:, columns] * ffn_scale
+        up_proj = up_total[:, columns] * ffn_scale
         active = gate_proj / (1.0 + jnp.exp(-gate_proj)) * up_proj
         hidden[:, columns] = active.astype(jnp.bfloat16)
 
@@ -270,8 +290,6 @@
         columns = aligned(i, TILE)
         product = jnp.dot(hidden[...], down[:, columns], preferred_element_type=jnp.float32)
         partials[columns, :] = (product.T * share).astype(jnp.bfloat16)
-
-    loop(0, full_width // TILE, narrow)
 
     mine = feature_block(partials)
 
@@ -293,44 +311,46 @@
             {"expert": target * 2 + y, "head": h},
         )
 
-    def core_order(k):
-        turned = lax.rem(z + 1 + lax.rem(k, z_size), z_size)
-        side = k // z_size
-        return turned, turned * 2 + lax.rem(1 - y + side, 2)
-
-    def core_start(k):
-        core_copy(core_order(k)[1]).start()
-
-    loop(0, n_expert, core_start)
-
     def core_add(expert):
         core_copy(expert).wait_recv()
         own = partials[aligned(expert * n_head + h, width), :].astype(jnp.float32)
         core_sums[expert] = (own + from_core[expert].astype(jnp.float32)).astype(jnp.bfloat16)
 
-    def core_send(k):
-        turned, expert = core_order(k)
-        core_add(expert)
-        y_copy(turned).start()
-
-    loop(0, z_size, core_send)
-
-    def core_keep(k):
-        core_add(core_order(k)[1])
-
-    loop(z_size, n_expert, core_keep)
-
     def y_add(k):
         y_copy(k).wait_recv()
         total = core_sums[k * 2 + y].astype(jnp.float32) + from_y[k].astype(jnp.float32)
         y_sums[k] = total.astype(jnp.bfloat16)
 
-    def y_send(k):
-        y_add(lax.rem(z + k, z_size))
-        z_copy(k).start()
-
-    loop(1, z_size, y_send)
-    y_add(z)
+    whole_tiles = group // TILE if group % TILE == 0 else 0
+    if not whole_tiles:
+        loop(0, full_width // TILE, narrow)
+
+    def scatter_step(k):
+        @pl.when(k <= z_size)
+        def _():
+            target = lax.rem(z + k, z_size)
+            if whole_tiles:
+                for part in range(whole_tiles):
+                    narrow(target * whole_tiles + part)
+            core_copy(target * 2 + 1 - y).start()
+            core_copy(target * 2 + y).start()
+
+        @pl.when(jnp.logical_and(k >= 2, k <= z_size + 1))
+        def _():
+            target = lax.rem(z + k - 1, z_size)
+            core_add(target * 2 + 1 - y)
+            y_copy(target).start()
+            core_add(target * 2 + y)
+
+        @pl.when(k >= 3)
+        def _():
+            y_add(lax.rem(z + k - 2, z_size))
+
+            @pl.when(k - 2 < z_size)
+            def _():
+                z_copy(k - 2).start()
+
+    loop(1, z_size + 3, scatter_step)
     total = stream[aligned(me, width), :].astype(jnp.float32) + y_sums[z].astype(jnp.float32)
 
     def z_add(k, total):
@@ -341,7 +361,13 @@
     layer_out = total.astype(jnp.bfloat16)
     layer_ref[...] = layer_out
     final_stream[aligned(me, width), :] = layer_out
-    gather(3, feature_block(final_stream))
+    clear(lm_squares, logit_total)
+    loads[3].wait()
+    gather(
+        3,
+        feature_block(final_stream),
+        multiply(final_stream, lm_gain_ref, lm_squares, ((vocab, logit_total),)),
+    )
 
     def summed(k):
         core_copy(k).wait_send()
@@ -350,13 +376,11 @@
     loop(0, z_size, lambda k: y_copy(k).wait_send())
     loop(1, z_size, lambda k: z_copy(k).wait_send())
 
-    normalise(final_stream, lm_gain_ref)
-    loads[3].wait()
+    lm_scale = lax.rsqrt(lm_squares[...] / full_width + 1e-05)
 
     def project(i):
         columns = aligned(i, TILE)
-        product = jnp.dot(rows_major[...], vocab[:, columns], preferred_element_type=jnp.float32)
-        logits[columns, :] = product.T
+        logits[columns, :] = (logit_total[:, columns] * lm_scale).T
 
     loop(0, logits.shape[0] // TILE, project)
     best = jnp.concatenate(best_of(logits, logits.shape[0] // 8, rows), axis=0)
@@ -417,7 +441,11 @@
             half16(n_head, n_expert * context.shape[0], context.shape[1]),
             half16(full_width, rows),
             half16(full_width, rows),
-            half16(rows, full_width),
+            pltpu.VMEM((rows, 1), jnp.float32),
+            pltpu.VMEM((rows, w_gate.shape[1]), jnp.float32),
+            pltpu.VMEM((rows, w_gate.shape[1]), jnp.float32),
+            pltpu.VMEM((rows, 1), jnp.float32),
+            pltpu.VMEM((rows, vocab_weight.shape[1]), jnp.float32),
             half16(rows, w_gate.shape[1]),
             half16(full_width, rows),
             half16(n_expert, width, rows),
@@ -437,13 +465,13 @@
         context,
         out_proj.T,
         hidden_in.T,
-        ffn_gain[None],
+        ffn_gain.reshape(n_expert // 2, 1, -1),
         routes.T,
         route_weights.T,
         w_gate,
         w_up,
         w_down,
-        lm_gain[None],
+        lm_gain.reshape(n_expert // 2, 1, -1),
         vocab_weight,
     )
     return (layer_t.T, best_t.T)

time: 84.1 us -> 84.6 us (level)
  no operation moved by 1% of the time
where the time goes in v2:
time: 84.6 us; the launch traced here: 84.1 us
  Pallas kernels  72.2 us (85%)
  local copies, waits for them, and re-layouts  6.86 us (8%)
  matrix products  2.61 us (3%)
  other arithmetic  1.77 us (2%)
    pallas_call x1, Pallas kernels, shards(): pl.pallas_call(functools.partial(layer_kernel, n_expert, n_head), out_sha...  72.2 us
    unnamed x4, local copies, waits for them, and re-layouts  3.02 us

profile of v2, /device:TPU:0, one launch (start us, length us, event | category | flops | bytes accessed | tf_op | source)
XLA Modules:
  0.0 84.1 jit_solution(13102491487462859311)
XLA Ops:
  0.6 0.0 copy-start
  0.6 0.7 compare_and_fusion
  1.4 0.3 copy-done
  1.7 0.6 gather_fusion
  2.3 0.7 broadcast_in_dim.30
  3.1 0.1 lt.23
  3.2 0.1 iota_compare_fusion
  3.2 1.3 %fusion.22 = (f32[16,2,6]{2,1,0:T(2,128)S(1)}, f32[16,2,6,64]{3,2,1,0:T(8,128)S(1)}) fusion(bf16[16,2,6,128]{3,1,2,0:T(2,128)(2,1)} %param.20, bf16[16,2,64,128]{3,2,1,0:T(8,128)(2,1)S(1)} %gather_fusion, pred[16]{0:T(512)(128)(4,1)S(1)} %get-tuple-element.7, pred[16,64]{1,0:T(8,128)(4,1)S(1)} %iota_compare_fusion), kind=kOutput, calls=%fused_computation.39 | convolution fusion | flops 3444544 | bytes 624400 | tf_op jit(solution)/shard_map/rgjd,rgtd->rgjt/dot_general | solution.py:24
  4.6 1.0 %fusion.10 = f32[16,2,1,6]{3,2,1,0:T(1,128)S(1)} fusion(bf16[16,2,6,128]{3,1,2,0:T(2,128)(2,1)} %param.20, bf16[16,2,128,1]{2,1,0,3:T(2,128)(2,1)} %bitcast.23), kind=kOutput, calls=%fused_computation.16 | convolution fusion | flops 49152 | bytes 58112 | tf_op jit(solution)/shard_map/rgjd,rgd->rgj/dot_general | solution.py:28
  5.6 0.2 fusion.9
  5.8 1.7 %gather_fusion.1 = bf16[16,2,64,128]{3,2,1,0:T(8,128)(2,1)S(1)} fusion(bf16[16,2,64,128]{3,2,1,0:T(8,128)(2,1)} %param.24, s32[1024]{0:T(1024)S(1)} %pad_clamp_fusion), kind=kCustom, calls=%fused_computation.1.clone | custom fusion | bytes 1048640 | tf_op jit(solution)/shard_map/jit(_take)/gather | solution.py:21
  7.5 0.7 convert_element_type.18
  8.2 0.3 fusion.2
  8.5 0.7 reshape.42.context_ref
  9.2 72.2 %shard_map.176 = (bf16[192,128]{1,0:T(8,128)(2,1)}, f32[8,128]{1,0:T(8,128)}) custom-call(bf16[16,1536]{1,0:T(8,128)(2,1)} %reshape.42.context_ref, bf16[192,3072]{1,0:T(8,128)(2,1)} %bitcast.13, bf16[192,128]{1,0:T(8,128)(2,1)} %bitcast.16, f32[4,1,768]{2,1,0:T(1,128)} %bitcast.18, s32[2,128]{1,0:T(2,128)} %bitcast.21, f32[2,128]{1,0:T(2,128)} %bitcast.22, ...), custom_call_target="tpu_custom_call" | custom-call | tf_op jit(solution)/shard_map/pallas_call | solution.py:427
  81.4 1.4 %copy.33 = bf16[128,192]{0,1:T(8,128)(2,1)} copy(bf16[128,192]{0,1:T(8,128)(2,1)} %bitcast.17) | data formatting | bytes 98304
  82.8 1.3 %copy.34 = f32[128,8]{0,1:T(8,128)} copy(f32[128,8]{0,1:T(8,128)} %bitcast.20) | data formatting | bytes 8192
  (3 shorter events, 0.1 us)
Async XLA Ops:
  0.6 1.1 %copy-start = (bf16[16,2,64,128]{3,2,1,0:T(8,128)(2,1)S(1)}, bf16[16,2,64,128]{3,2,1,0:T(8,128)(2,1)}, u32[]{:S(2)}) copy-start(bf16[16,2,64,128]{3,2,1,0:T(8,128)(2,1)} %param.23) | copy-start | bytes 1572868

commit v3 on v2

--- a/solution.py
+++ b/solution.py
@@ -51,6 +51,8 @@
 
 
 def aligned(index, size):
+    if isinstance(index, int):
+        return pl.ds(index * size, size)
     return pl.ds(pl.multiple_of(index * size, size), size)
 
 
@@ -64,7 +66,7 @@
         return tuple(result)
 
     lowest = jnp.full((8, width), -jnp.inf, jnp.float32)
-    kept = list(lax.fori_loop(0, groups, insert, (lowest,) * TOPK))
+    kept = list(lax.fori_loop(0, groups, insert, (lowest,) * TOPK, unroll=8))
     lane_class = lax.broadcasted_iota(jnp.int32, (8, width), 0)
     best = []
     for _ in range(TOPK):
@@ -248,14 +250,8 @@
             squares[...] += jnp.sum(block * block, axis=1, keepdims=True)
             block = (block * gain_ref[number]).astype(jnp.bfloat16)
 
-            def tile(i):
-                columns = aligned(i, TILE)
-                for weight, total in pairs:
-                    total[:, columns] += jnp.dot(
-                        block, weight[features, columns], preferred_element_type=jnp.float32
-                    )
-
-            loop(0, pairs[0][0].shape[1] // TILE, tile)
+            for weight, total in pairs:
+                total[...] += jnp.dot(block, weight[features, :], preferred_element_type=jnp.float32)
 
         return consume
 
@@ -277,7 +273,8 @@
         active = gate_proj / (1.0 + jnp.exp(-gate_proj)) * up_proj
         hidden[:, columns] = active.astype(jnp.bfloat16)
 
-    loop(0, hidden.shape[1] // TILE, widen)
+    for i in range(hidden.shape[1] // TILE):
+        widen(i)
     loads[2].wait()
     expert_here = me // (n_devices // E)
     share = jnp.sum(
@@ -382,7 +379,8 @@
         columns = aligned(i, TILE)
         logits[columns, :] = (logit_total[:, columns] * lm_scale).T
 
-    loop(0, logits.shape[0] // TILE, project)
+    for i in range(logits.shape[0] // TILE):
+        project(i)
     best = jnp.concatenate(best_of(logits, logits.shape[0] // 8, rows), axis=0)
     candidates[aligned(me, TOPK), :] = best
 

time: 84.6 us -> 76.3 us (0.902)
  Pallas kernels: 72.2 us -> 63.9 us
    pallas_call x1, Pallas kernels: 72.2 us -> 63.9 us  [shards(): pl.pallas_call(functools.partial(layer_kernel, n_expert, n_head), out_sha...]
where the time goes in v3:
time: 76.3 us; the launch traced here: 75.8 us
  Pallas kernels  63.9 us (84%)
  local copies, waits for them, and re-layouts  6.86 us (9%)
  matrix products  2.61 us (3%)
  other arithmetic  1.77 us (2%)
    pallas_call x1, Pallas kernels, shards(): pl.pallas_call(functools.partial(layer_kernel, n_expert, n_head), out_sha...  63.9 us
    unnamed x4, local copies, waits for them, and re-layouts  3.02 us
    gather x1, local copies, waits for them, and re-layouts, attend(): picked_values = jnp.take(cache_values, source, axis=0)  1.69 us

profile of v3, /device:TPU:0, one launch (start us, length us, event | category | flops | bytes accessed | tf_op | source)
XLA Modules:
  0.0 75.8 jit_solution(12623559318343815022)
XLA Ops:
  0.6 0.0 copy-start
  0.6 0.7 compare_and_fusion
  1.4 0.3 copy-done
  1.7 0.6 gather_fusion
  2.3 0.7 broadcast_in_dim.30
  3.1 0.1 lt.23
  3.2 0.1 iota_compare_fusion
  3.2 1.3 %fusion.22 = (f32[16,2,6]{2,1,0:T(2,128)S(1)}, f32[16,2,6,64]{3,2,1,0:T(8,128)S(1)}) fusion(bf16[16,2,6,128]{3,1,2,0:T(2,128)(2,1)} %param.20, bf16[16,2,64,128]{3,2,1,0:T(8,128)(2,1)S(1)} %gather_fusion, pred[16]{0:T(512)(128)(4,1)S(1)} %get-tuple-element.7, pred[16,64]{1,0:T(8,128)(4,1)S(1)} %iota_compare_fusion), kind=kOutput, calls=%fused_computation.39 | convolution fusion | flops 3444544 | bytes 624400 | tf_op jit(solution)/shard_map/rgjd,rgtd->rgjt/dot_general | solution.py:24
  4.6 1.0 %fusion.10 = f32[16,2,1,6]{3,2,1,0:T(1,128)S(1)} fusion(bf16[16,2,6,128]{3,1,2,0:T(2,128)(2,1)} %param.20, bf16[16,2,128,1]{2,1,0,3:T(2,128)(2,1)} %bitcast.23), kind=kOutput, calls=%fused_computation.16 | convolution fusion | flops 49152 | bytes 58112 | tf_op jit(solution)/shard_map/rgjd,rgd->rgj/dot_general | solution.py:28
  5.6 0.2 fusion.9
  5.8 1.7 %gather_fusion.1 = bf16[16,2,64,128]{3,2,1,0:T(8,128)(2,1)S(1)} fusion(bf16[16,2,64,128]{3,2,1,0:T(8,128)(2,1)} %param.24, s32[1024]{0:T(1024)S(1)} %pad_clamp_fusion), kind=kCustom, calls=%fused_computation.1.clone | custom fusion | bytes 1048640 | tf_op jit(solution)/shard_map/jit(_take)/gather | solution.py:21
  7.5 0.7 convert_element_type.18
  8.2 0.3 fusion.2
  8.5 0.7 reshape.42.context_ref
  9.2 63.9 %shard_map.176 = (bf16[192,128]{1,0:T(8,128)(2,1)}, f32[8,128]{1,0:T(8,128)}) custom-call(bf16[16,1536]{1,0:T(8,128)(2,1)} %reshape.42.context_ref, bf16[192,3072]{1,0:T(8,128)(2,1)} %bitcast.13, bf16[192,128]{1,0:T(8,128)(2,1)} %bitcast.16, f32[4,1,768]{2,1,0:T(1,128)} %bitcast.18, s32[2,128]{1,0:T(2,128)} %bitcast.21, f32[2,128]{1,0:T(2,128)} %bitcast.22, ...), custom_call_target="tpu_custom_call" | custom-call | tf_op jit(solution)/shard_map/pallas_call | solution.py:425
  73.2 1.4 %copy.33 = bf16[128,192]{0,1:T(8,128)(2,1)} copy(bf16[128,192]{0,1:T(8,128)(2,1)} %bitcast.17) | data formatting | bytes 98304
  74.6 1.3 %copy.34 = f32[128,8]{0,1:T(8,128)} copy(f32[128,8]{0,1:T(8,128)} %bitcast.20) | data formatting | bytes 8192
  (3 shorter events, 0.1 us)
Async XLA Ops:
  0.6 1.1 %copy-start = (bf16[16,2,64,128]{3,2,1,0:T(8,128)(2,1)S(1)}, bf16[16,2,64,128]{3,2,1,0:T(8,128)(2,1)}, u32[]{:S(2)}) copy-start(bf16[16,2,64,128]{3,2,1,0:T(8,128)(2,1)} %param.23) | copy-start | bytes 1572868

commit v4 on v3

--- a/solution.py
+++ b/solution.py
@@ -283,8 +283,8 @@
         keepdims=True,
     )
 
-    def narrow(i):
-        columns = aligned(i, TILE)
+    def narrow(i, size=TILE):
+        columns = aligned(i, size)
         product = jnp.dot(hidden[...], down[:, columns], preferred_element_type=jnp.float32)
         partials[columns, :] = (product.T * share).astype(jnp.bfloat16)
 
@@ -327,8 +327,7 @@
         def _():
             target = lax.rem(z + k, z_size)
             if whole_tiles:
-                for part in range(whole_tiles):
-                    narrow(target * whole_tiles + part)
+                narrow(target, group)
             core_copy(target * 2 + 1 - y).start()
             core_copy(target * 2 + y).start()
 

time: 76.3 us -> 76.3 us (level)
  no operation moved by 1% of the time
where the time goes in v4:
time: 76.3 us; the launch traced here: 75.8 us
  Pallas kernels  63.9 us (84%)
  local copies, waits for them, and re-layouts  6.86 us (9%)
  matrix products  2.61 us (3%)
  other arithmetic  1.77 us (2%)
    pallas_call x1, Pallas kernels, shards(): pl.pallas_call(functools.partial(layer_kernel, n_expert, n_head), out_sha...  63.9 us
    unnamed x4, local copies, waits for them, and re-layouts  3.02 us
    gather x1, local copies, waits for them, and re-layouts, attend(): picked_values = jnp.take(cache_values, source, axis=0)  1.69 us

profile of v4, /device:TPU:0, one launch (start us, length us, event | category | flops | bytes accessed | tf_op | source)
XLA Modules:
  0.0 75.8 jit_solution(14777724906428034690)
XLA Ops:
  0.6 0.0 copy-start
  0.6 0.7 compare_and_fusion
  1.4 0.3 copy-done
  1.7 0.6 gather_fusion
  2.3 0.7 broadcast_in_dim.30
  3.1 0.1 lt.23
  3.2 0.1 iota_compare_fusion
  3.2 1.3 %fusion.22 = (f32[16,2,6]{2,1,0:T(2,128)S(1)}, f32[16,2,6,64]{3,2,1,0:T(8,128)S(1)}) fusion(bf16[16,2,6,128]{3,1,2,0:T(2,128)(2,1)} %param.20, bf16[16,2,64,128]{3,2,1,0:T(8,128)(2,1)S(1)} %gather_fusion, pred[16]{0:T(512)(128)(4,1)S(1)} %get-tuple-element.7, pred[16,64]{1,0:T(8,128)(4,1)S(1)} %iota_compare_fusion), kind=kOutput, calls=%fused_computation.39 | convolution fusion | flops 3444544 | bytes 624400 | tf_op jit(solution)/shard_map/rgjd,rgtd->rgjt/dot_general | solution.py:24
  4.6 1.0 %fusion.10 = f32[16,2,1,6]{3,2,1,0:T(1,128)S(1)} fusion(bf16[16,2,6,128]{3,1,2,0:T(2,128)(2,1)} %param.20, bf16[16,2,128,1]{2,1,0,3:T(2,128)(2,1)} %bitcast.23), kind=kOutput, calls=%fused_computation.16 | convolution fusion | flops 49152 | bytes 58112 | tf_op jit(solution)/shard_map/rgjd,rgd->rgj/dot_general | solution.py:28
  5.6 0.2 fusion.9
  5.8 1.7 %gather_fusion.1 = bf16[16,2,64,128]{3,2,1,0:T(8,128)(2,1)S(1)} fusion(bf16[16,2,64,128]{3,2,1,0:T(8,128)(2,1)} %param.24, s32[1024]{0:T(1024)S(1)} %pad_clamp_fusion), kind=kCustom, calls=%fused_computation.1.clone | custom fusion | bytes 1048640 | tf_op jit(solution)/shard_map/jit(_take)/gather | solution.py:21
  7.5 0.7 convert_element_type.18
  8.2 0.3 fusion.2
  8.5 0.7 reshape.42.context_ref
  9.2 63.9 %shard_map.176 = (bf16[192,128]{1,0:T(8,128)(2,1)}, f32[8,128]{1,0:T(8,128)}) custom-call(bf16[16,1536]{1,0:T(8,128)(2,1)} %reshape.42.context_ref, bf16[192,3072]{1,0:T(8,128)(2,1)} %bitcast.13, bf16[192,128]{1,0:T(8,128)(2,1)} %bitcast.16, f32[4,1,768]{2,1,0:T(1,128)} %bitcast.18, s32[2,128]{1,0:T(2,128)} %bitcast.21, f32[2,128]{1,0:T(2,128)} %bitcast.22, ...), custom_call_target="tpu_custom_call" | custom-call | tf_op jit(solution)/shard_map/pallas_call | solution.py:424
  73.1 1.4 %copy.33 = bf16[128,192]{0,1:T(8,128)(2,1)} copy(bf16[128,192]{0,1:T(8,128)(2,1)} %bitcast.17) | data formatting | bytes 98304
  74.5 1.3 %copy.34 = f32[128,8]{0,1:T(8,128)} copy(f32[128,8]{0,1:T(8,128)} %bitcast.20) | data formatting | bytes 8192
  (3 shorter events, 0.1 us)
Async XLA Ops:
  0.6 1.1 %copy-start = (bf16[16,2,64,128]{3,2,1,0:T(8,128)(2,1)S(1)}, bf16[16,2,64,128]{3,2,1,0:T(8,128)(2,1)}, u32[]{:S(2)}) copy-start(bf16[16,2,64,128]{3,2,1,0:T(8,128)(2,1)} %param.23) | copy-start | bytes 1572868
